TPU v7x, 128 devices: a whole 4x4x4 slice. The times are simulated.
128 devices in a mesh: fsdp: 32 (over z, x, core), layer: 4 (over y).
Axes of the slice: x: 4, y: 4, z: 4, core: 2. Of those that a mesh axis runs over, the one named last changes fastest.
Arguments:
- gradients: bfloat16 [4, 256, 256, 256], P('layer', 'fsdp'), may hold values from -8 to 8
- second_moment: float32 [4, 256, 256, 256], P('layer', 'fsdp'), may hold values from 0.0001 to 0.01
- owners: int32 [4, 256, 1], P('layer'), may hold values from 0 to 31, as said below
- left_stats: float32 [4, 384, 256, 256], P('layer', 'fsdp'), may hold values from -0.3 to 4.3, as said below
- right_stats: float32 [4, 384, 256, 256], P('layer', 'fsdp'), may hold values from -0.3 to 4.3, as said below
- left_root: bfloat16 [4, 384, 256, 256], P('layer', 'fsdp'), may hold values from -0.3 to 1.8
- right_root: bfloat16 [4, 384, 256, 256], P('layer', 'fsdp'), may hold values from -0.3 to 1.8
Outputs:
- update: bfloat16 [4, 256, 256, 256], P('layer', 'fsdp')
- new_left_stats: float32 [4, 384, 256, 256], P('layer', 'fsdp')
- new_right_stats: float32 [4, 384, 256, 256], P('layer', 'fsdp')
Inputs may be any that keep to these rules, and one draw needn't show every extreme that they name: In the list of one matrix, the 8 blocks of one index of fsdp (blocks i * 8 to (i + 1) * 8 - 1) name distinct owners, and no owner is named more than 12 times; every owner keeps the statistics and roots of its k-th owned block (in list order) in its slot k, and slots past its count are unused. `left_stats`: Symmetric. `right_stats`: Symmetric.
All inputs are finite; a program needn't handle non-finite values.
Results may differ from a plain program's by a relative error of at most 0.0057.
Values may be sent and summed in bfloat16 or wider, within the bound.
A program may use at most 192 MiB of HBM per device.

v0:
```python
import jax
import jax.numpy as jnp
from jax import lax
from jax.sharding import PartitionSpec as P

ADAM_EPS = 1e-08
DECAY_RATE = 0.95
UPDATE_RMS = 1.0
NORM_FLOOR = 1e-06


def selection_tables(owner_list, owner_count, blocks, slots_here, my_index):
    total_blocks = owner_list.shape[0]
    owner_hot = (owner_list[:, None] == lax.iota(jnp.int32, owner_count)[None, :]).astype(
        jnp.float32
    )
    row_ids = lax.iota(jnp.int32, total_blocks)
    strict_lower = (row_ids[:, None] > row_ids[None, :]).astype(jnp.float32)
    before_all = jnp.dot(strict_lower, owner_hot, precision=lax.Precision.HIGHEST)
    slot_number = jnp.sum(before_all * owner_hot, axis=1)
    mine_mask = (owner_list == my_index).astype(jnp.float32)
    slot_hot = (slot_number[:, None] == lax.iota(jnp.float32, slots_here)[None, :]).astype(
        jnp.float32
    ) * mine_mask[:, None]
    home_hot = ((row_ids // blocks)[:, None] == lax.iota(jnp.int32, owner_count)[None, :]).astype(
        jnp.float32
    )
    return (owner_hot, home_hot, slot_hot)


def owner_work(gathered, left_stats, right_stats, left_root, right_root):
    gram_left = jnp.einsum("sij,skj->sik", gathered, gathered, preferred_element_type=jnp.float32)
    gram_right = jnp.einsum("sji,sjk->sik", gathered, gathered, preferred_element_type=jnp.float32)
    new_left = DECAY_RATE * left_stats[0] + (1.0 - DECAY_RATE) * gram_left
    new_right = DECAY_RATE * right_stats[0] + (1.0 - DECAY_RATE) * gram_right
    half_done = jnp.einsum(
        "sij,sjk->sik", left_root[0], gathered, preferred_element_type=jnp.float32
    ).astype(jnp.bfloat16)
    preconditioned = jnp.einsum(
        "sij,sjk->sik", half_done, right_root[0], preferred_element_type=jnp.float32
    ).astype(jnp.bfloat16)
    return (preconditioned, new_left[None], new_right[None])


def per_device(gradients, second_moment, owners, left_stats, right_stats, left_root, right_root):
    owner_count = lax.axis_size("fsdp")
    my_index = lax.axis_index("fsdp")
    blocks = gradients.shape[1]
    block_side = gradients.shape[3]
    slots_here = left_stats.shape[1]
    grad_local = gradients[0]
    owner_list = owners[0, :, 0]
    total_blocks = owner_list.shape[0]
    adam_dir = grad_local.astype(jnp.float32) / (jnp.sqrt(second_moment[0]) + ADAM_EPS)
    block_sq = jnp.sum(adam_dir * adam_dir, axis=(1, 2))
    global_sq = lax.psum(jnp.sum(block_sq), ("fsdp", "layer"))
    entry_count = float(total_blocks * lax.axis_size("layer") * block_side * block_side)
    clip_factor = jnp.minimum(1.0, UPDATE_RMS / jnp.sqrt(global_sq / entry_count))
    owner_hot, home_hot, slot_hot = selection_tables(
        owner_list, owner_count, blocks, slots_here, my_index
    )
    first_row = my_index * blocks
    my_owner_hot = lax.dynamic_slice_in_dim(owner_hot, first_row, blocks, 0).astype(jnp.bfloat16)
    outgoing = jnp.einsum(
        "jo,jxy->oxy", my_owner_hot, grad_local, preferred_element_type=jnp.float32
    ).astype(jnp.bfloat16)
    received = lax.all_to_all(outgoing, "fsdp", split_axis=0, concat_axis=0, tiled=True)
    pick_table = jnp.einsum("bs,bh->sh", slot_hot, home_hot).astype(jnp.bfloat16)
    gathered = jnp.einsum(
        "sh,hxy->sxy", pick_table, received, preferred_element_type=jnp.float32
    ).astype(jnp.bfloat16)
    preconditioned, new_left, new_right = owner_work(
        gathered, left_stats, right_stats, left_root, right_root
    )
    answers = jnp.einsum(
        "sh,sxy->hxy", pick_table, preconditioned, preferred_element_type=jnp.float32
    ).astype(jnp.bfloat16)
    returned = lax.all_to_all(answers, "fsdp", split_axis=0, concat_axis=0, tiled=True)
    home_blocks = jnp.einsum(
        "jo,oxy->jxy", my_owner_hot, returned, preferred_element_type=jnp.float32
    )
    pre_float = home_blocks.astype(jnp.bfloat16).astype(jnp.float32)
    graft_ratio = jnp.sqrt(block_sq / float(block_side * block_side)) / jnp.sqrt(
        jnp.sum(pre_float * pre_float, axis=(1, 2)) / float(block_side * block_side) + NORM_FLOOR
    )
    update = (pre_float * (graft_ratio * clip_factor)[:, None, None]).astype(jnp.bfloat16)
    return (update[None], new_left, new_right)


def solution(mesh):
    return jax.shard_map(
        per_device,
        mesh=mesh,
        in_specs=(
            P("layer", "fsdp", None, None),
            P("layer", "fsdp", None, None),
            P("layer", None, None),
            P("layer", "fsdp", None, None),
            P("layer", "fsdp", None, None),
            P("layer", "fsdp", None, None),
            P("layer", "fsdp", None, None),
        ),
        out_specs=(
            P("layer", "fsdp", None, None),
            P("layer", "fsdp", None, None),
            P("layer", "fsdp", None, None),
        ),
        check_vma=False,
    )
```

profile of v0, /device:TPU:1, one launch (start us, length us, event | category | flops | bytes accessed | tf_op | source)
XLA Modules:
  0.0 215.1 jit_solution(2232057942751181500)
XLA Ops:
  0.6 0.0 copy-start
  0.7 0.8 iota_compare_fusion.6
  1.5 2.5 %convolution_convert_fusion.1 = bf16[32,256,256]{2,0,1:T(8,128)(2,1)S(1)} fusion(bf16[8,256,256]{2,1,0:T(8,128)(2,1)} %bitcast.48, pred[256,32]{0,1:T(32,128)(4,1)S(1)} %iota_compare_fusion.6, s32[]{:T(128)S(6)} %select_n.12), kind=kOutput, calls=%fused_computation.10 | convolution fusion | flops 35652096 | bytes 5246980 | tf_op jit(solution)/shard_map/jo,jxy->oxy/dot_general | solution.py:64
  4.0 4.4 %copy.24 = bf16[32,256,256]{2,1,0:T(8,128)(2,1)} copy(bf16[32,256,256]{2,0,1:T(8,128)(2,1)S(1)} %convolution_convert_fusion.1) | data formatting | bytes 8388608 | tf_op jit(solution)/shard_map/convert_element_type | solution.py:66
  8.4 0.0 copy-start.4
  8.4 9.6 %all-to-all-start = ((bf16[32,256,256]{2,1,0:T(8,128)(2,1)}), bf16[32,256,256]{2,1,0:T(8,128)(2,1)}, u32[]{:S(2)}, u32[]{:S(2)}) async-start(bf16[32,256,256]{2,1,0:T(8,128)(2,1)} %copy.24), calls=%async_computation | async-start | bytes 8388608 | tf_op jit(solution)/shard_map/all_to_all | solution.py:67
  18.0 0.0 copy-done.4
  18.0 0.2 fusion.17
  18.3 0.3 fusion.18
  18.5 49.6 %all-to-all-done = bf16[32,256,256]{2,1,0:T(8,128)(2,1)} async-done(((bf16[32,256,256]{2,1,0:T(8,128)(2,1)}), bf16[32,256,256]{2,1,0:T(8,128)(2,1)}, u32[]{:S(2)}, u32[]{:S(2)}) %all-to-all-start) | async-done | bytes 4194336 | tf_op jit(solution)/shard_map/all_to_all | solution.py:67
  68.2 5.9 %fusion.2 = bf16[12,256,256]{2,0,1:T(8,128)(2,1)} fusion(bf16[12,32,1]{1,0,2:T(8,128)(2,1)S(1)} %fusion.18, bf16[32,256,256]{2,1,0:T(8,128)(2,1)} %all-to-all-done), kind=kOutput, calls=%fused_computation.2 | convolution fusion | flops 50331648 | bytes 5767936 | tf_op jit(solution)/shard_map/sh,hxy->sxy/dot_general | solution.py:69
  74.1 0.0 copy-done
  74.1 3.6 %convolution_convert_fusion.2 = bf16[12,256,256]{2,1,0:T(8,128)(2,1)S(1)} fusion(bf16[1,12,256,256]{3,2,1,0:T(8,128)(2,1)S(1)} %copy-done, bf16[1,12,256,256]{3,2,1,0:T(8,128)(2,1)} %param.12, bf16[12,256,256]{2,0,1:T(8,128)(2,1)} %fusion.2), kind=kOutput, calls=%fused_computation.18 | convolution fusion | flops 806879232 | bytes 6291456 | tf_op jit(solution)/shard_map/sij,sjk->sik/dot_general | solution.py:39
  77.8 1.3 convolution_convert_fusion
  79.0 4.4 %copy.30 = bf16[32,256,256]{2,1,0:T(8,128)(2,1)} copy(bf16[32,256,256]{2,0,1:T(8,128)(2,1)S(1)} %convolution_convert_fusion) | data formatting | bytes 8388608 | tf_op jit(solution)/shard_map/convert_element_type | solution.py:77
  83.4 0.0 copy-start.2
  83.4 8.2 %all-to-all-start.1 = ((bf16[32,256,256]{2,1,0:T(8,128)(2,1)}), bf16[32,256,256]{2,1,0:T(8,128)(2,1)}, u32[]{:S(2)}, u32[]{:S(2)}) async-start(bf16[32,256,256]{2,1,0:T(8,128)(2,1)} %copy.30), calls=%async_computation.1 | async-start | bytes 8388608 | tf_op jit(solution)/shard_map/all_to_all | solution.py:78
  91.6 0.0 copy-done.2
  91.6 3.7 %fusion.32 = (f32[]{:T(128)}, f32[8]{0:T(128)S(1)}) fusion(f32[1,8,256,256]{3,2,1,0:T(8,128)} %param.8, bf16[1,8,256,256]{3,2,1,0:T(8,128)(2,1)S(1)} %copy-done.2), kind=kLoop, calls=%fused_computation.49 | loop fusion | flops 3145719 | bytes 3145764 | tf_op jit(solution)/shard_map/reduce_sum | solution.py:56
  95.3 102.8 %psum.7 = f32[]{:T(128)} all-reduce(f32[]{:T(128)} %get-tuple-element.12), channel_id=1, replica_groups=mesh['fsdp'=32,'layer'=4] {'fsdp','layer'}, use_global_device_ids=true, to_apply=%region_4.5 | all-reduce | flops 1 | bytes 8 | tf_op jit(solution)/shard_map/psum | solution.py:56
  198.8 0.0 copy-start.1
  198.8 0.0 copy-start.3
  198.8 6.9 %fusion.4 = f32[1,12,256,256]{3,2,1,0:T(8,128)} fusion(f32[1,12,256,256]{3,2,1,0:T(8,128)} %param.11, bf16[12,256,256]{2,0,1:T(8,128)(2,1)} %fusion.2), kind=kOutput, calls=%fused_computation.5 | convolution fusion | flops 405012480 | bytes 7864320 | tf_op jit(solution)/shard_map/sji,sjk->sik/dot_general | solution.py:33
  205.7 0.0 copy-done.1
  205.7 0.0 copy-done.3
  205.7 3.0 %fusion.5 = f32[1,12,256,256]{3,2,1,0:T(8,128)} fusion(f32[1,12,256,256]{3,2,1,0:T(8,128)S(1)} %copy-done.3, bf16[12,256,256]{2,0,1:T(8,128)(2,1)S(1)} %copy-done.1), kind=kOutput, calls=%fused_computation.7 | convolution fusion | flops 405012480 | bytes 7864320 | tf_op jit(solution)/shard_map/sij,skj->sik/dot_general | solution.py:32
  208.7 0.0 all-to-all-done.1
  208.7 4.7 %fusion.6 = (f32[8]{0:T(128)S(1)}, bf16[8,256,256]{2,0,1:T(8,128)(2,1)S(1)}) fusion(bf16[32,256,256]{2,1,0:T(8,128)(2,1)} %all-to-all-done.1, pred[256,32]{0,1:T(32,128)(4,1)S(1)} %iota_compare_fusion.6, s32[]{:T(128)S(6)} %select_n.12), kind=kOutput, calls=%fused_computation.13 | convolution fusion | flops 35652088 | bytes 5247012 | tf_op jit(solution)/shard_map/jo,oxy->jxy/dot_general | solution.py:79
  213.5 0.5 fusion.19
  213.9 1.2 copy.34
  (3 shorter events, 0.0 us)
Async XLA Ops:
  0.6 73.5 %copy-start = (bf16[1,12,256,256]{3,2,1,0:T(8,128)(2,1)S(1)}, bf16[1,12,256,256]{3,2,1,0:T(8,128)(2,1)}, u32[]{:S(2)}) copy-start(bf16[1,12,256,256]{3,2,1,0:T(8,128)(2,1)} %param.13) | copy-start | bytes 4718596
  8.4 9.6 %copy-start.4 = (s32[1,256,1]{1,2,0:T(1,128)S(1)}, s32[1,256,1]{1,2,0:T(1,128)}, u32[]{:S(2)}) copy-start(s32[1,256,1]{1,2,0:T(1,128)} %param.9) | copy-start | bytes 3076
  8.4 59.8 %all-to-all-start = ((bf16[32,256,256]{2,1,0:T(8,128)(2,1)}), bf16[32,256,256]{2,1,0:T(8,128)(2,1)}, u32[]{:S(2)}, u32[]{:S(2)}) async-start(bf16[32,256,256]{2,1,0:T(8,128)(2,1)} %copy.24), calls=%async_computation | async-start | bytes 8388608 | tf_op jit(solution)/shard_map/all_to_all | solution.py:67
  83.4 8.2 %copy-start.2 = (bf16[1,8,256,256]{3,2,1,0:T(8,128)(2,1)S(1)}, bf16[1,8,256,256]{3,2,1,0:T(8,128)(2,1)}, u32[]{:S(2)}) copy-start(bf16[1,8,256,256]{3,2,1,0:T(8,128)(2,1)} %param.7) | copy-start | bytes 3145732
  83.4 125.3 %all-to-all-start.1 = ((bf16[32,256,256]{2,1,0:T(8,128)(2,1)}), bf16[32,256,256]{2,1,0:T(8,128)(2,1)}, u32[]{:S(2)}, u32[]{:S(2)}) async-start(bf16[32,256,256]{2,1,0:T(8,128)(2,1)} %copy.30), calls=%async_computation.1 | async-start | bytes 8388608 | tf_op jit(solution)/shard_map/all_to_all | solution.py:78
  198.8 6.9 %copy-start.1 = (bf16[12,256,256]{2,0,1:T(8,128)(2,1)S(1)}, bf16[12,256,256]{2,0,1:T(8,128)(2,1)}, u32[]{:S(2)}) copy-start(bf16[12,256,256]{2,0,1:T(8,128)(2,1)} %fusion.2) | copy-start | bytes 4718596
  198.8 6.9 %copy-start.3 = (f32[1,12,256,256]{3,2,1,0:T(8,128)S(1)}, f32[1,12,256,256]{3,2,1,0:T(8,128)}, u32[]{:S(2)}) copy-start(f32[1,12,256,256]{3,2,1,0:T(8,128)} %param.10) | copy-start | bytes 9437188
where the time goes:
time: 216 us; the launch traced here: 215 us
  blocking collectives  103 us (48%)
  waiting for transfers between devices  49.6 us (23%)
  matrix products  28.5 us (13%)
  starting transfers between devices  17.8 us (8%)
  local copies, waits for them, and re-layouts  9.98 us (5%)
  other arithmetic  4.97 us (2%)
    psum x1, blocking collectives, per_device(): global_sq = lax.psum(jnp.sum(block_sq), ('fsdp', 'layer'))  103 us
    all_to_all x1, waiting for transfers between devices, per_device(): lax.all_to_all(outgoing, 'fsdp', split_axis=0, concat_axis=0, tiled=True)  49.6 us
    all_to_all x1, starting transfers between devices, per_device(): lax.all_to_all(outgoing, 'fsdp', split_axis=0, concat_axis=0, tiled=True)  9.63 us
    all_to_all x1, starting transfers between devices, per_device(): lax.all_to_all(answers, 'fsdp', split_axis=0, concat_axis=0, tiled=True)  8.19 us
    dot_general x1, matrix products, owner_work(): jnp.einsum('sji,sjk->sik', gathered, gathered, preferred_element_type=jnp...  6.89 us
    dot_general x1, matrix products, per_device(): jnp.einsum('sh,hxy->sxy', pick_table, received, preferred_element_type=jn...  5.94 us
    dot_general x1, matrix products, per_device(): jnp.einsum('jo,oxy->jxy', my_owner_hot, returned, preferred_element_type=...  4.73 us
    convert_element_type x1, local copies, waits for them, and re-layouts, per_device(): outgoing = jnp.einsum('jo,jxy->oxy', my_owner_hot, grad_local, preferred_...  4.39 us
  transfers between devices with their start and end apart: 2, of which 1 were waited for; matrix products, arithmetic and copies ran while one was open for 7% of the time, Pallas kernels for 0%

commit v1 on v0

v1 whole, which is shorter than its diff:
```python
import functools

import jax
import jax.numpy as jnp
from jax import lax
from jax.experimental import pallas as pl
from jax.experimental.pallas import tpu as pltpu
from jax.sharding import PartitionSpec as P

ADAM_EPS = 1e-08
DECAY_RATE = 0.95
UPDATE_RMS = 1.0
NORM_FLOOR = 1e-06

MESH = pl.DeviceIdType.MESH
RING = 4
CORES = 2
N = RING * RING * CORES
LAYERS = 4
BS = 256
BLOCKS = 8
NB = N * BLOCKS
CAP = 12
ROWS = 16
LANES = 128
GROUPS = 3
PER = CAP // GROUPS
MIB = 2**20


def hops(step):
    dz, dx, _ = step
    return min(dz, RING - dz) + min(dx, RING - dx)


STEPS = sorted(
    (
        (dz, dx, dc)
        for dz in range(RING)
        for dx in range(RING)
        for dc in range(CORES)
        if (dz, dx, dc) != (0, 0, 0)
    ),
    key=lambda step: -hops(step),
)


def partner(me, step):
    dz, dx, dc = step
    z, x, c = me // (RING * CORES), (me // CORES) % RING, me % CORES
    return ((z + dz) % RING * RING + (x + dx) % RING) * CORES + (c + dc) % CORES


def piece(ref, k):
    rows = pl.ds(pl.multiple_of((k // 2) * ROWS, ROWS), ROWS)
    return ref.at[:, k % 2, rows, :]


def wait_bytes(ref, sem):
    pltpu.make_async_copy(ref, ref, sem).wait()


def routed_kernel(
    take_ref, back_ref, grad_ref, second_ref, left_ref, right_ref,
    owned_ref, home_ref, norms_ref,
    grad, second, left, right, spread, outgo, answer, arrived, homing, sums, totals,
    load_sems, self_sems, send_sems, route_sems, recv_sems, sum_sems,
):
    me = lax.axis_index("fsdp")
    layer = lax.axis_index("layer")

    barrier = pltpu.get_barrier_semaphore()
    for step in STEPS:
        pl.semaphore_signal(
            barrier, inc=1, device_id={"fsdp": partner(me, step)}, device_id_type=MESH
        )
    for offset in range(1, LAYERS):
        pl.semaphore_signal(
            barrier,
            inc=1,
            device_id={"layer": (layer + offset) % LAYERS},
            device_id_type=MESH,
        )
    loads = [
        pltpu.make_async_copy(
            grad_ref.at[0, :, :, pl.ds(half * LANES, LANES)], grad.at[:, half], load_sems.at[half]
        )
        for half in range(2)
    ]
    loads.append(pltpu.make_async_copy(second_ref.at[0], second, load_sems.at[2]))
    loads.append(pltpu.make_async_copy(left_ref.at[0], left, load_sems.at[3]))
    loads.append(pltpu.make_async_copy(right_ref.at[0], right, load_sems.at[4]))
    for load in loads:
        load.start()
    spread[NB] = jnp.zeros((ROWS, LANES), jnp.bfloat16)
    loads[0].wait()
    loads[1].wait()
    pl.semaphore_wait(barrier, N - 1 + LAYERS - 1)

    def remote(src, dst, send_sem, recv_sem, target):
        copy = pltpu.make_async_remote_copy(
            src_ref=src,
            dst_ref=dst,
            send_sem=send_sem,
            recv_sem=recv_sem,
            device_id={"fsdp": target},
            device_id_type=MESH,
        )
        copy.start()

    my_blocks = pl.ds(me * BLOCKS, BLOCKS)
    for step in STEPS:
        target = partner(me, step)
        remote(piece(grad, target), spread.at[my_blocks], send_sems.at[0], recv_sems.at[0], target)
    own = pltpu.make_async_copy(piece(grad, me), spread.at[my_blocks], self_sems.at[0])
    own.start()

    loads[2].wait()

    def adam_block(b, total):
        row_sum = jnp.zeros((8, LANES), jnp.float32)
        for half in range(2):
            for quarter in range(4):
                rows = pl.ds(quarter * 64, 64)
                lanes = pl.ds(half * LANES, LANES)
                direction = grad[b, half, rows, :].astype(jnp.float32) / (
                    jnp.sqrt(second[b, rows, lanes]) + ADAM_EPS
                )
                row_sum += jnp.sum((direction * direction).reshape(8, 8, LANES), axis=0)
        block_sum = jnp.full((8, LANES), jnp.sum(row_sum), jnp.float32)
        norms_ref[b] = block_sum
        return total + block_sum

    sums[N - 1] = lax.fori_loop(0, BLOCKS, adam_block, jnp.zeros((8, LANES), jnp.float32))

    own.wait()
    wait_bytes(spread.at[pl.ds(0, NB - BLOCKS)], recv_sems.at[0])

    for group in range(GROUPS):

        def take(target, carry):
            for slot in range(PER):
                row = spread[take_ref[target * CAP + group * PER + slot]]
                outgo[group, target * PER + slot] = row
            return carry

        lax.fori_loop(0, N, take, 0)
        place = owned_ref.at[pl.ds(group * PER, PER)]
        for step in STEPS:
            target = partner(me, step)
            remote(
                outgo.at[group, pl.ds(target * PER, PER)],
                piece(place, me),
                send_sems.at[1],
                route_sems.at[group],
                target,
            )
        pltpu.make_async_copy(
            outgo.at[group, pl.ds(me * PER, PER)], piece(place, me), self_sems.at[1 + group]
        ).start()

    for index, step in enumerate(STEPS):
        remote(sums.at[N - 1], sums.at[index], send_sems.at[4], sum_sems.at[0], partner(me, step))

    loads[3].wait()
    loads[4].wait()
    for group in range(GROUPS):
        place = owned_ref.at[pl.ds(group * PER, PER)]
        wait_bytes(outgo.at[group, pl.ds(0, PER * (N - 1))], route_sems.at[group])
        pltpu.make_async_copy(
            outgo.at[group, pl.ds(me * PER, PER)], piece(place, me), self_sems.at[1 + group]
        ).wait()

        def precondition(index, carry):
            slot = group * PER + index
            block = jnp.concatenate([owned_ref[slot, 0], owned_ref[slot, 1]], axis=1)
            half_done = jnp.dot(
                left[slot], block, preferred_element_type=jnp.float32
            ).astype(jnp.bfloat16)
            full = jnp.dot(
                half_done, right[slot], preferred_element_type=jnp.float32
            ).astype(jnp.bfloat16)
            answer[slot, 0] = full[:, :LANES]
            answer[slot, 1] = full[:, LANES:]
            return carry

        lax.fori_loop(0, PER, precondition, 0)
        done = answer.at[pl.ds(group * PER, PER)]
        landing = arrived.at[pl.ds(me * CAP + group * PER, PER)]
        for step in STEPS:
            target = partner(me, step)
            remote(piece(done, target), landing, send_sems.at[2], recv_sems.at[1], target)
        pltpu.make_async_copy(piece(done, me), landing, self_sems.at[4]).start()

    wait_bytes(sums.at[pl.ds(0, N - 1)], sum_sems.at[0])
    totals[LAYERS - 1] = jnp.sum(sums[...], axis=0)
    for offset in range(1, LAYERS):
        pltpu.make_async_remote_copy(
            src_ref=totals.at[LAYERS - 1],
            dst_ref=totals.at[offset - 1],
            send_sem=send_sems.at[5],
            recv_sem=sum_sems.at[1],
            device_id={"layer": (layer + offset) % LAYERS},
            device_id_type=MESH,
        ).start()

    wait_bytes(arrived.at[pl.ds(0, CAP)], self_sems.at[4])
    wait_bytes(arrived.at[pl.ds(0, CAP * (N - 1))], recv_sems.at[1])

    def give(target, carry):
        for block in range(BLOCKS):
            homing[target * BLOCKS + block] = arrived[back_ref[target * BLOCKS + block]]
        return carry

    lax.fori_loop(0, N, give, 0)
    for step in STEPS:
        target = partner(me, step)
        remote(
            homing.at[pl.ds(target * BLOCKS, BLOCKS)],
            piece(home_ref, me),
            send_sems.at[3],
            recv_sems.at[2],
            target,
        )
    own = pltpu.make_async_copy(homing.at[my_blocks], piece(home_ref, me), self_sems.at[5])
    own.start()

    wait_bytes(totals.at[pl.ds(0, LAYERS - 1)], sum_sems.at[1])
    norms_ref[BLOCKS] = jnp.sum(totals[...], axis=0)
    own.wait()
    wait_bytes(homing.at[pl.ds(0, NB - BLOCKS)], recv_sems.at[2])
    wait_bytes(homing.at[pl.ds(0, NB - BLOCKS)], send_sems.at[3])
    wait_bytes(spread.at[pl.ds(0, NB - BLOCKS)], send_sems.at[0])
    wait_bytes(arrived.at[pl.ds(0, CAP * (N - 1))], send_sems.at[1])
    wait_bytes(arrived.at[pl.ds(0, CAP * (N - 1))], send_sems.at[2])
    wait_bytes(sums.at[pl.ds(0, N - 1)], send_sems.at[4])
    wait_bytes(totals.at[pl.ds(0, LAYERS - 1)], send_sems.at[5])


def routed(take_table, back_table, gradients, second_moment, left_root, right_root):
    bf16, f32 = jnp.bfloat16, jnp.float32
    smem = pl.BlockSpec(memory_space=pltpu.SMEM)
    vmem = pl.BlockSpec(memory_space=pltpu.VMEM)
    hbm = pl.BlockSpec(memory_space=pl.ANY)
    return pl.pallas_call(
        routed_kernel,
        out_shape=(
            jax.ShapeDtypeStruct((CAP, 2, BS, LANES), bf16),
            jax.ShapeDtypeStruct((BLOCKS, 2, BS, LANES), bf16),
            jax.ShapeDtypeStruct((BLOCKS + 1, 8, LANES), f32),
        ),
        in_specs=[smem, smem, hbm, hbm, hbm, hbm],
        out_specs=(vmem, vmem, vmem),
        scratch_shapes=[
            pltpu.VMEM((BLOCKS, 2, BS, LANES), bf16),
            pltpu.VMEM((BLOCKS, BS, BS), f32),
            pltpu.VMEM((CAP, BS, BS), bf16),
            pltpu.VMEM((CAP, BS, BS), bf16),
            pltpu.VMEM((NB + 1, ROWS, LANES), bf16),
            pltpu.VMEM((GROUPS, N * PER, ROWS, LANES), bf16),
            pltpu.VMEM((CAP, 2, BS, LANES), bf16),
            pltpu.VMEM((N * CAP, ROWS, LANES), bf16),
            pltpu.VMEM((NB, ROWS, LANES), bf16),
            pltpu.VMEM((N, 8, LANES), f32),
            pltpu.VMEM((LAYERS, 8, LANES), f32),
            pltpu.SemaphoreType.DMA((5,)),
            pltpu.SemaphoreType.DMA((6,)),
            pltpu.SemaphoreType.DMA((6,)),
            pltpu.SemaphoreType.DMA((GROUPS,)),
            pltpu.SemaphoreType.DMA((3,)),
            pltpu.SemaphoreType.DMA((2,)),
        ],
        compiler_params=pltpu.CompilerParams(
            collective_id=0, has_side_effects=True, vmem_limit_bytes=32 * MIB
        ),
        cost_estimate=pl.CostEstimate(
            flops=2 * 2 * CAP * BS**3, bytes_accessed=10 * MIB, transcendentals=0
        ),
        name="route_blocks",
    )(take_table, back_table, gradients, second_moment, left_root, right_root)


SLOTS_STEP = 3
BLOCKS_STEP = 2


def finish_kernel(owned_ref, home_ref, norms_ref, total_ref, left_ref, right_ref,
                  update_ref, new_left_ref, new_right_ref):
    for slot in range(SLOTS_STEP):
        block = jnp.concatenate([owned_ref[slot, 0], owned_ref[slot, 1]], axis=1)
        gram_left = lax.dot_general(
            block, block, (((1,), (1,)), ((), ())), preferred_element_type=jnp.float32
        )
        gram_right = lax.dot_general(
            block, block, (((0,), (0,)), ((), ())), preferred_element_type=jnp.float32
        )
        new_left_ref[0, slot] = DECAY_RATE * left_ref[0, slot] + (1.0 - DECAY_RATE) * gram_left
        new_right_ref[0, slot] = DECAY_RATE * right_ref[0, slot] + (1.0 - DECAY_RATE) * gram_right
    entries = float(LAYERS * NB * BS * BS)
    clip_factor = jnp.minimum(1.0, UPDATE_RMS / jnp.sqrt(total_ref[0, :1, :] / entries))
    for block in range(BLOCKS_STEP):
        pre = home_ref[block].astype(jnp.float32)
        pre_sq = jnp.full((1, LANES), jnp.sum(pre * pre), jnp.float32)
        ratio = jnp.sqrt(norms_ref[block, :1, :] / float(BS * BS)) / jnp.sqrt(
            pre_sq / float(BS * BS) + NORM_FLOOR
        )
        factor = ratio * clip_factor
        for half in range(2):
            update_ref[0, block, :, half * LANES : (half + 1) * LANES] = (
                pre[half] * factor
            ).astype(jnp.bfloat16)


def finish(owned, home, norms, left_stats, right_stats):
    def slots(*tail):
        return pl.BlockSpec((1, SLOTS_STEP) + tail, lambda i: (0, i, 0, 0))

    def blocks(n, *tail):
        return pl.BlockSpec((n,) + tail, lambda i: (i,) + (0,) * len(tail))

    return pl.pallas_call(
        finish_kernel,
        grid=(CAP // SLOTS_STEP,),
        out_shape=(
            jax.ShapeDtypeStruct((1, BLOCKS, BS, BS), jnp.bfloat16),
            jax.ShapeDtypeStruct((1, CAP, BS, BS), jnp.float32),
            jax.ShapeDtypeStruct((1, CAP, BS, BS), jnp.float32),
        ),
        in_specs=[
            blocks(SLOTS_STEP, 2, BS, LANES),
            blocks(BLOCKS_STEP, 2, BS, LANES),
            blocks(BLOCKS_STEP, 8, LANES),
            pl.BlockSpec((1, 8, LANES), lambda i: (BLOCKS, 0, 0)),
            slots(BS, BS),
            slots(BS, BS),
        ],
        out_specs=(
            pl.BlockSpec((1, BLOCKS_STEP, BS, BS), lambda i: (0, i, 0, 0)),
            slots(BS, BS),
            slots(BS, BS),
        ),
        compiler_params=pltpu.CompilerParams(vmem_limit_bytes=24 * MIB),
        cost_estimate=pl.CostEstimate(
            flops=2 * 2 * CAP * BS**3, bytes_accessed=16 * MIB, transcendentals=0
        ),
        name="finish_stats",
    )(owned, home, norms, norms, left_stats, right_stats)


def slot_tables(owner_list):
    rows = lax.iota(jnp.int32, NB)
    same = owner_list[:, None] == owner_list[None, :]
    earlier = jnp.sum((same & (rows[:, None] > rows[None, :])).astype(jnp.int32), axis=1)
    slot_index = owner_list * CAP + earlier
    hit = lax.iota(jnp.int32, N * CAP)[:, None] == slot_index[None, :]
    take = NB + jnp.sum(jnp.where(hit, rows[None, :] - NB, 0), axis=1)
    return take, slot_index


def per_device(gradients, second_moment, owners, left_stats, right_stats, left_root, right_root):
    take_table, back_table = slot_tables(owners[0, :, 0])
    owned, home, norms = routed(
        take_table, back_table, gradients, second_moment, left_root, right_root
    )
    return finish(owned, home, norms, left_stats, right_stats)


def solution(mesh):
    blocked = P("layer", "fsdp", None, None)
    return jax.shard_map(
        per_device,
        mesh=mesh,
        in_specs=(blocked, blocked, P("layer", None, None), blocked, blocked, blocked, blocked),
        out_specs=(blocked, blocked, blocked),
        check_vma=False,
    )
```

time: 216 us -> 87 us (0.40)
  blocking collectives: 103 us -> 0 us
  Pallas kernels: 0 us -> 78.7 us
  waiting for transfers between devices: 49.6 us -> 0 us
  matrix products: 28.5 us -> 0 us
  starting transfers between devices: 17.8 us -> 0 us
  local copies, waits for them, and re-layouts: 9.98 us -> 5.64 us
  other arithmetic: 4.97 us -> 1.77 us
    psum x1 -> x0, blocking collectives: 103 us -> none  [per_device(): global_sq = lax.psum(jnp.sum(block_sq), ('fsdp', 'layer'))]
    pallas_call x0 -> x2, Pallas kernels: none -> 78.7 us  [the longest x1 74.5 us: routed(): pl.pallas_call(routed_kernel, out_shape=(jax.ShapeDtypeStruct((CAP, 2, BS...]
    all_to_all x2 -> x0, waiting for transfers between devices: 49.6 us -> none  [the longest x1 49.6 us: per_device(): lax.all_to_all(outgoing, 'fsdp', split_axis=0, concat_axis=0, tiled=True)]
    dot_general x9 -> x0, matrix products: 28.5 us -> none  [the longest x1 6.89 us: owner_work(): jnp.einsum('sji,sjk->sik', gathered, gathered, preferred_element_type=jnp...]
    all_to_all x2 -> x0, starting transfers between devices: 17.8 us -> none  [the longest x1 9.63 us: per_device(): lax.all_to_all(outgoing, 'fsdp', split_axis=0, concat_axis=0, tiled=True)]
    convert_element_type x2 -> x0, local copies, waits for them, and re-layouts: 8.78 us -> none  [the longest x1 4.39 us: per_device(): outgoing = jnp.einsum('jo,jxy->oxy', my_owner_hot, grad_local, preferred_...]
    unnamed x11 -> x12, local copies, waits for them, and re-layouts: 1.21 us -> 5.64 us
    reduce_sum x1 -> x2, other arithmetic: 3.65 us -> 1.08 us  [the longest x1 0.93 us: slot_tables(): jnp.sum((same & (rows[:, None] > rows[None, :])).astype(jnp.int32), axis=1)]
  transfers between devices with their start and end apart: 2 -> 0, of which waited for: 1 -> 0; matrix products, arithmetic and copies ran while one was open for 7% -> 0% of each run, Pallas kernels for 0% -> 0%
where the time goes in v1:
time: 87 us; the launch traced here: 86.7 us
  Pallas kernels  78.7 us (90%)
  local copies, waits for them, and re-layouts  5.64 us (6%)
  other arithmetic  1.77 us (2%)
    pallas_call x1, Pallas kernels, routed(): pl.pallas_call(routed_kernel, out_shape=(jax.ShapeDtypeStruct((CAP, 2, BS...  74.5 us
    unnamed x12, local copies, waits for them, and re-layouts  5.64 us
    pallas_call x1, Pallas kernels, finish(): pl.pallas_call(finish_kernel, grid=(CAP // SLOTS_STEP,), out_shape=(jax.S...  4.14 us

profile of v1, /device:TPU:1, one launch (start us, length us, event | category | flops | bytes accessed | tf_op | source)
XLA Modules:
  0.0 86.7 jit_solution(10316317201750757726)
XLA Ops:
  0.6 0.9 %convert_reduce_fusion = s32[256]{0:T(256)S(1)} fusion(s32[256]{0:T(256)} %bitcast.1), kind=kLoop, calls=%fused_computation.2 | loop fusion | flops 327424 | bytes 2048 | tf_op jit(solution)/shard_map/reduce_sum | solution.py:353
  1.6 0.7 iota_add_fusion
  2.3 0.1 select_reduce_fusion
  2.4 0.0 copy-start.2
  2.4 1.6 %copy-done.2 = f32[1,8,256,256]{3,2,1,0:T(8,128)S(1)} copy-done((f32[1,8,256,256]{3,2,1,0:T(8,128)S(1)}, f32[1,8,256,256]{3,2,1,0:T(8,128)}, u32[]{:S(2)}) %copy-start.2) | copy-done | bytes 2097176
  4.0 0.0 copy-start.3
  4.0 1.4 %copy-done.3 = bf16[1,12,256,256]{3,2,1,0:T(8,128)(2,1)S(1)} copy-done((bf16[1,12,256,256]{3,2,1,0:T(8,128)(2,1)S(1)}, bf16[1,12,256,256]{3,2,1,0:T(8,128)(2,1)}, u32[]{:S(2)}) %copy-start.3) | copy-done | bytes 1572888
  5.4 0.0 copy-start.4
  5.4 1.4 %copy-done.4 = bf16[1,12,256,256]{3,2,1,0:T(8,128)(2,1)S(1)} copy-done((bf16[1,12,256,256]{3,2,1,0:T(8,128)(2,1)S(1)}, bf16[1,12,256,256]{3,2,1,0:T(8,128)(2,1)}, u32[]{:S(2)}) %copy-start.4) | copy-done | bytes 1572888
  6.8 0.0 copy-start.5
  6.8 1.2 %copy-done.5 = bf16[1,8,256,256]{3,2,1,0:T(8,128)(2,1)S(1)} copy-done((bf16[1,8,256,256]{3,2,1,0:T(8,128)(2,1)S(1)}, bf16[1,8,256,256]{3,2,1,0:T(8,128)(2,1)}, u32[]{:S(2)}) %copy-start.5) | copy-done | bytes 1048600
  8.0 0.0 copy-start
  8.0 0.0 copy-start.1
  8.0 74.5 %route_blocks.1 = (bf16[12,2,256,128]{3,2,1,0:T(8,128)(2,1)S(1)}, bf16[8,2,256,128]{3,2,1,0:T(8,128)(2,1)S(1)}, f32[9,8,128]{2,1,0:T(8,128)S(1)}) custom-call(s32[384]{0:T(512)S(1)} %broadcast_add_fusion.take_ref, s32[256]{0:T(256)S(1)} %get-tuple-element.10.back_ref, bf16[1,8,256,256]{3,2,1,0:T(8,128)(2,1)S(1)} %copy-done.5, ...), custom_call_target="tpu_custom_call" | custom-call | flops 805306368 | bytes 10485760 | tf_op jit(solution)/shard_map/route_blocks/pallas_call | solution.py:245
  82.6 0.0 copy-done
  82.6 0.0 copy-done.1
  82.6 4.1 %finish_stats.1 = (bf16[1,8,256,256]{3,2,1,0:T(8,128)(2,1)}, f32[1,12,256,256]{3,2,1,0:T(8,128)}, f32[1,12,256,256]{3,2,1,0:T(8,128)}) custom-call(bf16[12,2,256,128]{3,2,1,0:T(8,128)(2,1)S(1)} %get-tuple-element.6.owned_ref, bf16[8,2,256,128]{3,2,1,0:T(8,128)(2,1)S(1)} %get-tuple-element.7.home_ref, f32[9,8,128]{2,1,0:T(8,128)S(1)} %get-tuple-element.8.norms_ref.total_ref, ...), custom_call_target="tpu_custom_call" | custom-call | flops 805306368 | bytes 16777216 | tf_op jit(solution)/shard_map/finish_stats/pallas_call | solution.py:321
  (1 shorter events, 0.0 us)
Async XLA Ops:
  2.4 1.6 %copy-start.2 = (f32[1,8,256,256]{3,2,1,0:T(8,128)S(1)}, f32[1,8,256,256]{3,2,1,0:T(8,128)}, u32[]{:S(2)}) copy-start(f32[1,8,256,256]{3,2,1,0:T(8,128)} %second_ref.1) | copy-start | bytes 6291460
  4.0 1.4 %copy-start.3 = (bf16[1,12,256,256]{3,2,1,0:T(8,128)(2,1)S(1)}, bf16[1,12,256,256]{3,2,1,0:T(8,128)(2,1)}, u32[]{:S(2)}) copy-start(bf16[1,12,256,256]{3,2,1,0:T(8,128)(2,1)} %left_ref.2) | copy-start | bytes 4718596
  5.4 1.4 %copy-start.4 = (bf16[1,12,256,256]{3,2,1,0:T(8,128)(2,1)S(1)}, bf16[1,12,256,256]{3,2,1,0:T(8,128)(2,1)}, u32[]{:S(2)}) copy-start(bf16[1,12,256,256]{3,2,1,0:T(8,128)(2,1)} %right_ref.2) | copy-start | bytes 4718596
  6.8 1.2 %copy-start.5 = (bf16[1,8,256,256]{3,2,1,0:T(8,128)(2,1)S(1)}, bf16[1,8,256,256]{3,2,1,0:T(8,128)(2,1)}, u32[]{:S(2)}) copy-start(bf16[1,8,256,256]{3,2,1,0:T(8,128)(2,1)} %grad_ref.1) | copy-start | bytes 3145732
  8.0 74.5 %copy-start = (f32[1,12,256,256]{3,2,1,0:T(8,128)S(1)}, f32[1,12,256,256]{3,2,1,0:T(8,128)}, u32[]{:S(2)}) copy-start(f32[1,12,256,256]{3,2,1,0:T(8,128)} %left_ref.3) | copy-start | bytes 9437188
  8.0 74.5 %copy-start.1 = (f32[1,12,256,256]{3,2,1,0:T(8,128)S(1)}, f32[1,12,256,256]{3,2,1,0:T(8,128)}, u32[]{:S(2)}) copy-start(f32[1,12,256,256]{3,2,1,0:T(8,128)} %right_ref.3) | copy-start | bytes 9437188

commit v2 on v1

v2 whole, which is shorter than its diff:
```python
import jax
import jax.numpy as jnp
from jax import lax
from jax.experimental import pallas as pl
from jax.experimental.pallas import tpu as pltpu
from jax.sharding import PartitionSpec as P

ADAM_EPS = 1e-08
DECAY_RATE = 0.95
UPDATE_RMS = 1.0
NORM_FLOOR = 1e-06

MESH = pl.DeviceIdType.MESH
RING = 4
CORES = 2
N = RING * RING * CORES
LAYERS = 4
BS = 256
BLOCKS = 8
NB = N * BLOCKS
CAP = 12
ROWS = 16
LANES = 128
GROUPS = 3
PER = CAP // GROUPS
MIB = 2**20


def hops(step):
    dz, dx, _ = step
    return min(dz, RING - dz) + min(dx, RING - dx)


STEPS = sorted(
    (
        (dz, dx, dc)
        for dz in range(RING)
        for dx in range(RING)
        for dc in range(CORES)
        if (dz, dx, dc) != (0, 0, 0)
    ),
    key=lambda step: (-hops(step), step[2], min(step[0], RING - step[0]), step),
)


def partner(me, step):
    dz, dx, dc = step
    z, x, c = me // (RING * CORES), (me // CORES) % RING, me % CORES
    return ((z + dz) % RING * RING + (x + dx) % RING) * CORES + (c + dc) % CORES


def by_core(me):
    z, x = me // (RING * CORES), (me // CORES) % RING
    places = [step[:2] for step in STEPS if step[2] == 0]

    def on_core(core):
        return [((z + dz) % RING * RING + (x + dx) % RING) * CORES + core for dz, dx in places]

    return on_core(0) + [partner(me, (0, 0, 1))] + on_core(1)


def piece_place(k):
    if isinstance(k, int):
        return pl.ds((k // 2) * ROWS, ROWS), pl.ds((k % 2) * LANES, LANES)
    rows = pl.ds(pl.multiple_of((k // 2) * ROWS, ROWS), ROWS)
    return rows, pl.ds(pl.multiple_of((k % 2) * LANES, LANES), LANES)


def join(pieces):
    return jnp.concatenate(
        [
            jnp.concatenate([pieces(2 * r + half) for r in range(BS // ROWS)], axis=0)
            for half in range(2)
        ],
        axis=1,
    )


def wait_bytes(ref, sem):
    pltpu.make_async_copy(ref, ref, sem).wait()


def slot_tables(owner_row):
    rows = lax.broadcasted_iota(jnp.int32, (NB, NB), 0)
    columns = lax.broadcasted_iota(jnp.int32, (NB, NB), 1)

    def upright(row):
        return jnp.sum(jnp.where(rows == columns, row, 0), axis=1, keepdims=True)

    same = (upright(owner_row) == owner_row) & (rows < columns)
    slot_index = owner_row * CAP + jnp.sum(jnp.where(same, 1, 0), axis=0, keepdims=True)
    slots = lax.broadcasted_iota(jnp.int32, (NB, N * CAP), 1)
    blocks = lax.broadcasted_iota(jnp.int32, (NB, N * CAP), 0)
    hit = upright(slot_index) == slots
    taken = NB + jnp.sum(jnp.where(hit, blocks - NB, 0), axis=0, keepdims=True)
    return taken, slot_index


def routed_kernel(
    owner_ref, grad_ref, second_ref, left_root_ref, right_root_ref, left_stats_ref, right_stats_ref,
    new_left_ref, new_right_ref, home_ref, norms_ref,
    owner_row, grad, second, left_root, right_root, left_stats, right_stats,
    leaving, spread, outgo, landed, owned, answer, arrived, homing, sums, totals,
    take_rows, back_rows, take_table, back_table,
    load_sems, table_sems, send_sems, route_sems, recv_sems, sum_sems,
):
    me = lax.axis_index("fsdp")
    layer = lax.axis_index("layer")

    barrier = pltpu.get_barrier_semaphore()
    for step in STEPS:
        pl.semaphore_signal(
            barrier, inc=1, device_id={"fsdp": partner(me, step)}, device_id_type=MESH
        )
    for offset in range(1, LAYERS):
        pl.semaphore_signal(
            barrier,
            inc=1,
            device_id={"layer": (layer + offset) % LAYERS},
            device_id_type=MESH,
        )
    loads = [
        pltpu.make_async_copy(src, dst, load_sems.at[index])
        for index, (src, dst) in enumerate(
            (
                (grad_ref.at[0], grad),
                (owner_ref, owner_row),
                (second_ref.at[0], second),
                (left_root_ref.at[0], left_root),
                (right_root_ref.at[0], right_root),
                (left_stats_ref.at[0], left_stats),
                (right_stats_ref.at[0], right_stats),
            )
        )
    ]
    loads[0].start()
    loads[1].start()
    loads[0].wait()
    pl.semaphore_wait(barrier, N - 1 + LAYERS - 1)

    def remote(src, dst, send_sem, recv_sem, target):
        copy = pltpu.make_async_remote_copy(
            src_ref=src,
            dst_ref=dst,
            send_sem=send_sem,
            recv_sem=recv_sem,
            device_id={"fsdp": target},
            device_id_type=MESH,
        )
        copy.start()

    targets = [partner(me, step) for step in STEPS]
    my_blocks = pl.ds(me * BLOCKS, BLOCKS)

    for target in by_core(me):
        leaving[target] = grad[(slice(None),) + piece_place(target)]
        remote(
            leaving.at[target], spread.at[my_blocks], send_sems.at[0], recv_sems.at[0], target
        )
    spread[my_blocks] = grad[(slice(None),) + piece_place(me)]
    spread[NB] = jnp.zeros((ROWS, LANES), jnp.bfloat16)

    for load in loads[2:]:
        load.start()
    loads[1].wait()
    take_rows[...], back_rows[...] = slot_tables(owner_row[...])
    tables = [
        pltpu.make_async_copy(take_rows, take_table, table_sems.at[0]),
        pltpu.make_async_copy(back_rows, back_table, table_sems.at[1]),
    ]
    for table in tables:
        table.start()
    for table in tables:
        table.wait()
    wait_bytes(spread.at[pl.ds(0, NB - BLOCKS)], recv_sems.at[0])

    def take(ref, group, target):
        for slot in range(PER):
            ref[group, target, slot] = spread[take_table[0, target * CAP + group * PER + slot]]

    for group in range(GROUPS):
        for target in targets:
            take(outgo, group, target)
            remote(
                outgo.at[group, target],
                landed.at[group, me],
                send_sems.at[1],
                route_sems.at[group],
                target,
            )
        take(landed, group, me)

    loads[3].wait()
    loads[4].wait()
    for group in range(GROUPS):
        wait_bytes(landed.at[group, pl.ds(0, N - 1)], route_sems.at[group])

        def precondition(index, carry):
            slot = group * PER + index
            block = join(lambda k: landed[group, k, index])
            owned[slot] = block
            half_done = jnp.dot(
                left_root[slot], block, preferred_element_type=jnp.float32
            ).astype(jnp.bfloat16)
            full = jnp.dot(
                half_done, right_root[slot], preferred_element_type=jnp.float32
            ).astype(jnp.bfloat16)
            for k in range(N):
                r, half = divmod(k, 2)
                answer[group, k, index] = full[
                    r * ROWS : (r + 1) * ROWS, half * LANES : (half + 1) * LANES
                ]
            return carry

        lax.fori_loop(0, PER, precondition, 0)
        landing = pl.ds(me * CAP + group * PER, PER)
        for target in by_core(me):
            remote(
                answer.at[group, target],
                arrived.at[landing],
                send_sems.at[2],
                recv_sems.at[1],
                target,
            )
        arrived[landing] = answer[group, me]

    loads[2].wait()

    def adam_block(b, total):
        row_sum = jnp.zeros((8, LANES), jnp.float32)
        for half in range(2):
            for quarter in range(4):
                rows = pl.ds(quarter * 64, 64)
                lanes = pl.ds(half * LANES, LANES)
                direction = grad[b, rows, lanes].astype(jnp.float32) / (
                    jnp.sqrt(second[b, rows, lanes]) + ADAM_EPS
                )
                row_sum += jnp.sum((direction * direction).reshape(8, 8, LANES), axis=0)
        block_sum = jnp.full((8, LANES), jnp.sum(row_sum), jnp.float32)
        norms_ref[b] = block_sum
        return total + block_sum

    sums[N - 1] = lax.fori_loop(0, BLOCKS, adam_block, jnp.zeros((8, LANES), jnp.float32))

    for index, target in enumerate(targets):
        remote(sums.at[N - 1], sums.at[index], send_sems.at[4], sum_sems.at[0], target)

    wait_bytes(arrived.at[pl.ds(0, CAP * (N - 1))], recv_sems.at[1])

    def give(ref, target):
        for block in range(BLOCKS):
            ref[target, block] = arrived[back_table[0, target * BLOCKS + block]]

    for target in targets:
        give(homing, target)
        remote(homing.at[target], home_ref.at[me], send_sems.at[3], recv_sems.at[2], target)
    give(home_ref, me)

    loads[5].wait()
    loads[6].wait()

    def statistics(slot, carry):
        block = owned[slot]
        gram_left = lax.dot_general(
            block, block, (((1,), (1,)), ((), ())), preferred_element_type=jnp.float32
        )
        gram_right = lax.dot_general(
            block, block, (((0,), (0,)), ((), ())), preferred_element_type=jnp.float32
        )
        new_left_ref[slot] = DECAY_RATE * left_stats[slot] + (1.0 - DECAY_RATE) * gram_left
        new_right_ref[slot] = DECAY_RATE * right_stats[slot] + (1.0 - DECAY_RATE) * gram_right
        return carry

    lax.fori_loop(0, CAP // 2, statistics, 0)

    wait_bytes(sums.at[pl.ds(0, N - 1)], sum_sems.at[0])
    totals[LAYERS - 1] = jnp.sum(sums[...], axis=0)
    for offset in range(1, LAYERS):
        pltpu.make_async_remote_copy(
            src_ref=totals.at[LAYERS - 1],
            dst_ref=totals.at[offset - 1],
            send_sem=send_sems.at[5],
            recv_sem=sum_sems.at[1],
            device_id={"layer": (layer + offset) % LAYERS},
            device_id_type=MESH,
        ).start()
    lax.fori_loop(CAP // 2, CAP, statistics, 0)

    wait_bytes(totals.at[pl.ds(0, LAYERS - 1)], sum_sems.at[1])
    norms_ref[BLOCKS] = jnp.sum(totals[...], axis=0)
    wait_bytes(leaving.at[pl.ds(0, N - 1)], send_sems.at[0])
    wait_bytes(arrived.at[pl.ds(0, CAP * (N - 1))], send_sems.at[1])
    wait_bytes(arrived.at[pl.ds(0, CAP * (N - 1))], send_sems.at[2])
    wait_bytes(sums.at[pl.ds(0, N - 1)], send_sems.at[4])
    wait_bytes(totals.at[pl.ds(0, LAYERS - 1)], send_sems.at[5])
    wait_bytes(homing.at[pl.ds(0, N - 1)], send_sems.at[3])
    wait_bytes(home_ref.at[pl.ds(0, N - 1)], recv_sems.at[2])


def routed(owner_row, gradients, second_moment, left_root, right_root, left_stats, right_stats):
    bf16, f32 = jnp.bfloat16, jnp.float32
    vmem = pl.BlockSpec(memory_space=pltpu.VMEM)
    hbm = pl.BlockSpec(memory_space=pltpu.HBM)
    operands = [
        pltpu.with_memory_space_constraint(array, pltpu.HBM)
        for array in (
            owner_row, gradients, second_moment, left_root, right_root, left_stats, right_stats
        )
    ]
    return pl.pallas_call(
        routed_kernel,
        out_shape=(
            pltpu.VMEM((CAP, BS, BS), f32),
            pltpu.VMEM((CAP, BS, BS), f32),
            pltpu.VMEM((N, BLOCKS, ROWS, LANES), bf16),
            pltpu.VMEM((BLOCKS + 1, 8, LANES), f32),
        ),
        in_specs=[hbm] * len(operands),
        out_specs=(vmem,) * 4,
        scratch_shapes=[
            pltpu.VMEM((1, NB), jnp.int32),
            pltpu.VMEM((BLOCKS, BS, BS), bf16),
            pltpu.VMEM((BLOCKS, BS, BS), f32),
            pltpu.VMEM((CAP, BS, BS), bf16),
            pltpu.VMEM((CAP, BS, BS), bf16),
            pltpu.VMEM((CAP, BS, BS), f32),
            pltpu.VMEM((CAP, BS, BS), f32),
            pltpu.VMEM((N, BLOCKS, ROWS, LANES), bf16),
            pltpu.VMEM((NB + 1, ROWS, LANES), bf16),
            pltpu.VMEM((GROUPS, N, PER, ROWS, LANES), bf16),
            pltpu.VMEM((GROUPS, N, PER, ROWS, LANES), bf16),
            pltpu.VMEM((CAP, BS, BS), bf16),
            pltpu.VMEM((GROUPS, N, PER, ROWS, LANES), bf16),
            pltpu.VMEM((N * CAP, ROWS, LANES), bf16),
            pltpu.VMEM((N, BLOCKS, ROWS, LANES), bf16),
            pltpu.VMEM((N, 8, LANES), f32),
            pltpu.VMEM((LAYERS, 8, LANES), f32),
            pltpu.VMEM((1, N * CAP), jnp.int32),
            pltpu.VMEM((1, NB), jnp.int32),
            pltpu.SMEM((1, N * CAP), jnp.int32),
            pltpu.SMEM((1, NB), jnp.int32),
            pltpu.SemaphoreType.DMA((7,)),
            pltpu.SemaphoreType.DMA((2,)),
            pltpu.SemaphoreType.DMA((6,)),
            pltpu.SemaphoreType.DMA((GROUPS,)),
            pltpu.SemaphoreType.DMA((3,)),
            pltpu.SemaphoreType.DMA((2,)),
        ],
        compiler_params=pltpu.CompilerParams(
            collective_id=0, has_side_effects=True, vmem_limit_bytes=34 * MIB
        ),
        cost_estimate=pl.CostEstimate(
            flops=4 * 2 * CAP * BS**3, bytes_accessed=18 * MIB, transcendentals=0
        ),
        name="route_blocks",
    )(*operands)


def finish_kernel(left_ref, right_ref, home_ref, norms_ref,
                  update_ref, new_left_ref, new_right_ref, update, sems):
    outs = [
        pltpu.make_async_copy(left_ref, new_left_ref.at[0], sems.at[0]),
        pltpu.make_async_copy(right_ref, new_right_ref.at[0], sems.at[1]),
    ]
    for out in outs:
        out.start()
    entries = float(LAYERS * NB * BS * BS)
    clip_factor = jnp.minimum(1.0, UPDATE_RMS / jnp.sqrt(norms_ref[BLOCKS, :1, :] / entries))
    for block in range(BLOCKS):
        pre = home_ref[:, block].astype(jnp.float32)
        pre_sq = jnp.full((1, LANES), jnp.sum(pre * pre), jnp.float32)
        ratio = jnp.sqrt(norms_ref[block, :1, :] / float(BS * BS)) / jnp.sqrt(
            pre_sq / float(BS * BS) + NORM_FLOOR
        )
        factor = ratio * clip_factor
        for k in range(N):
            update[(block,) + piece_place(k)] = (pre[k] * factor).astype(jnp.bfloat16)
    out = pltpu.make_async_copy(update, update_ref.at[0], sems.at[2])
    out.start()
    for copy in outs + [out]:
        copy.wait()


def finish(new_left, new_right, home, norms):
    vmem = pl.BlockSpec(memory_space=pltpu.VMEM)
    hbm = pl.BlockSpec(memory_space=pltpu.HBM)
    return pl.pallas_call(
        finish_kernel,
        out_shape=(
            jax.ShapeDtypeStruct((1, BLOCKS, BS, BS), jnp.bfloat16),
            jax.ShapeDtypeStruct((1, CAP, BS, BS), jnp.float32),
            jax.ShapeDtypeStruct((1, CAP, BS, BS), jnp.float32),
        ),
        in_specs=[vmem] * 4,
        out_specs=(hbm,) * 3,
        scratch_shapes=[
            pltpu.VMEM((BLOCKS, BS, BS), jnp.bfloat16),
            pltpu.SemaphoreType.DMA((3,)),
        ],
        compiler_params=pltpu.CompilerParams(vmem_limit_bytes=8 * MIB),
        cost_estimate=pl.CostEstimate(
            flops=6 * BLOCKS * BS * BS, bytes_accessed=14 * MIB, transcendentals=0
        ),
        name="write_results",
    )(new_left, new_right, home, norms)


def per_device(gradients, second_moment, owners, left_stats, right_stats, left_root, right_root):
    owner_row = owners.reshape(1, NB)
    new_left, new_right, home, norms = routed(
        owner_row, gradients, second_moment, left_root, right_root, left_stats, right_stats
    )
    return finish(new_left, new_right, home, norms)


def solution(mesh):
    blocked = P("layer", "fsdp", None, None)
    return jax.shard_map(
        per_device,
        mesh=mesh,
        in_specs=(blocked, blocked, P("layer", None, None), blocked, blocked, blocked, blocked),
        out_specs=(blocked, blocked, blocked),
        check_vma=False,
    )
```

time: 87 us -> 73.9 us (0.85)
  local copies, waits for them, and re-layouts: 5.64 us -> 0 us
  Pallas kernels: 78.7 us -> 73.1 us
  other arithmetic: 1.77 us -> 0 us
    unnamed x12 -> x0, local copies, waits for them, and re-layouts: 5.64 us -> none
    pallas_call x2, Pallas kernels: 78.7 us -> 73.1 us  [the longest x1 70.1 us: routed(): pl.pallas_call(routed_kernel, out_shape=(pltpu.VMEM((CAP, BS, BS), f32),...]
    reduce_sum x2 -> x0, other arithmetic: 1.08 us -> none  [the longest x1 0.93 us: slot_tables(): jnp.sum((same & (rows[:, None] > rows[None, :])).astype(jnp.int32), axis=1)]
where the time goes in v2:
time: 73.9 us; the launch traced here: 73.8 us
  Pallas kernels  73.1 us (99%)
    pallas_call x1, Pallas kernels, routed(): pl.pallas_call(routed_kernel, out_shape=(pltpu.VMEM((CAP, BS, BS), f32),...  70.1 us
    pallas_call x1, Pallas kernels, finish(): pl.pallas_call(finish_kernel, out_shape=(jax.ShapeDtypeStruct((1, BLOCKS,...  3.07 us

profile of v2, /device:TPU:1, one launch (start us, length us, event | category | flops | bytes accessed | tf_op | source)
XLA Modules:
  0.0 73.8 jit_solution(12329138281347201252)
XLA Ops:
  0.6 70.1 %route_blocks.1 = (f32[12,256,256]{2,1,0:T(8,128)S(1)}, f32[12,256,256]{2,1,0:T(8,128)S(1)}, bf16[32,8,16,128]{3,2,1,0:T(8,128)(2,1)S(1)}, f32[9,8,128]{2,1,0:T(8,128)S(1)}) custom-call(s32[1,256]{1,0:T(1,128)} %bitcast.1, bf16[1,8,256,256]{3,2,1,0:T(8,128)(2,1)} %grad_ref.1, f32[1,8,256,256]{3,2,1,0:T(8,128)} %second_ref.1, ...), custom_call_target="tpu_custom_call" | custom-call | flops 1610612736 | bytes 18874368 | tf_op jit(solution)/shard_map/route_blocks/pallas_call | solution.py:310
  70.7 3.1 %write_results.1 = (bf16[1,8,256,256]{3,2,1,0:T(8,128)(2,1)}, f32[1,12,256,256]{3,2,1,0:T(8,128)}, f32[1,12,256,256]{3,2,1,0:T(8,128)}) custom-call(f32[12,256,256]{2,1,0:T(8,128)S(1)} %get-tuple-element.7.left_ref, f32[12,256,256]{2,1,0:T(8,128)S(1)} %get-tuple-element.8.right_ref, bf16[32,8,16,128]{3,2,1,0:T(8,128)(2,1)S(1)} %get-tuple-element.9.home_ref, ...), custom_call_target="tpu_custom_call" | custom-call | flops 3145728 | bytes 14680064 | tf_op jit(solution)/shard_map/write_results/pallas_call | solution.py:387

commit v3 on v2

--- a/solution.py
+++ b/solution.py
@@ -56,7 +56,7 @@
     def on_core(core):
         return [((z + dz) % RING * RING + (x + dx) % RING) * CORES + core for dz, dx in places]
 
-    return on_core(0) + [partner(me, (0, 0, 1))] + on_core(1)
+    return on_core(0), on_core(1)
 
 
 def piece_place(k):
@@ -152,7 +152,9 @@
     targets = [partner(me, step) for step in STEPS]
     my_blocks = pl.ds(me * BLOCKS, BLOCKS)
 
-    for target in by_core(me):
+    to_core = by_core(me)
+    sibling = partner(me, (0, 0, 1))
+    for target in to_core[0] + [sibling] + to_core[1]:
         leaving[target] = grad[(slice(None),) + piece_place(target)]
         remote(
             leaving.at[target], spread.at[my_blocks], send_sems.at[0], recv_sems.at[0], target
@@ -170,6 +172,24 @@
     ]
     for table in tables:
         table.start()
+    loads[2].wait()
+
+    def adam_block(b, total):
+        row_sum = jnp.zeros((8, LANES), jnp.float32)
+        for half in range(2):
+            for quarter in range(4):
+                rows = pl.ds(quarter * 64, 64)
+                lanes = pl.ds(half * LANES, LANES)
+                direction = grad[b, rows, lanes].astype(jnp.float32) / (
+                    jnp.sqrt(second[b, rows, lanes]) + ADAM_EPS
+                )
+                row_sum += jnp.sum((direction * direction).reshape(8, 8, LANES), axis=0)
+        block_sum = jnp.full((1, LANES), jnp.sum(row_sum), jnp.float32)
+        norms_ref[b] = block_sum
+        return total + block_sum
+
+    sums[N - 1] = lax.fori_loop(0, BLOCKS, adam_block, jnp.zeros((1, LANES), jnp.float32))
+
     for table in tables:
         table.wait()
     wait_bytes(spread.at[pl.ds(0, NB - BLOCKS)], recv_sems.at[0])
@@ -190,10 +210,28 @@
             )
         take(landed, group, me)
 
+    for index, target in enumerate(targets):
+        remote(sums.at[N - 1], sums.at[index], send_sems.at[4], sum_sems.at[0], target)
+
     loads[3].wait()
     loads[4].wait()
+    def send_answers(group, core):
+        landing = pl.ds(me * CAP + group * PER, PER)
+        for target in to_core[core] + ([sibling] if core == 0 else []):
+            remote(
+                answer.at[group, target],
+                arrived.at[landing],
+                send_sems.at[2],
+                recv_sems.at[1],
+                target,
+            )
+        if core == 0:
+            arrived[landing] = answer[group, me]
+
     for group in range(GROUPS):
         wait_bytes(landed.at[group, pl.ds(0, N - 1)], route_sems.at[group])
+        if group > 0:
+            send_answers(group - 1, 0)
 
         def precondition(index, carry):
             slot = group * PER + index
@@ -213,65 +251,10 @@
             return carry
 
         lax.fori_loop(0, PER, precondition, 0)
-        landing = pl.ds(me * CAP + group * PER, PER)
-        for target in by_core(me):
-            remote(
-                answer.at[group, target],
-                arrived.at[landing],
-                send_sems.at[2],
-                recv_sems.at[1],
-                target,
-            )
-        arrived[landing] = answer[group, me]
-
-    loads[2].wait()
-
-    def adam_block(b, total):
-        row_sum = jnp.zeros((8, LANES), jnp.float32)
-        for half in range(2):
-            for quarter in range(4):
-                rows = pl.ds(quarter * 64, 64)
-                lanes = pl.ds(half * LANES, LANES)
-                direction = grad[b, rows, lanes].astype(jnp.float32) / (
-                    jnp.sqrt(second[b, rows, lanes]) + ADAM_EPS
-                )
-                row_sum += jnp.sum((direction * direction).reshape(8, 8, LANES), axis=0)
-        block_sum = jnp.full((8, LANES), jnp.sum(row_sum), jnp.float32)
-        norms_ref[b] = block_sum
-        return total + block_sum
-
-    sums[N - 1] = lax.fori_loop(0, BLOCKS, adam_block, jnp.zeros((8, LANES), jnp.float32))
-
-    for index, target in enumerate(targets):
-        remote(sums.at[N - 1], sums.at[index], send_sems.at[4], sum_sems.at[0], target)
-
-    wait_bytes(arrived.at[pl.ds(0, CAP * (N - 1))], recv_sems.at[1])
-
-    def give(ref, target):
-        for block in range(BLOCKS):
-            ref[target, block] = arrived[back_table[0, target * BLOCKS + block]]
-
-    for target in targets:
-        give(homing, target)
-        remote(homing.at[target], home_ref.at[me], send_sems.at[3], recv_sems.at[2], target)
-    give(home_ref, me)
-
-    loads[5].wait()
-    loads[6].wait()
-
-    def statistics(slot, carry):
-        block = owned[slot]
-        gram_left = lax.dot_general(
-            block, block, (((1,), (1,)), ((), ())), preferred_element_type=jnp.float32
-        )
-        gram_right = lax.dot_general(
-            block, block, (((0,), (0,)), ((), ())), preferred_element_type=jnp.float32
-        )
-        new_left_ref[slot] = DECAY_RATE * left_stats[slot] + (1.0 - DECAY_RATE) * gram_left
-        new_right_ref[slot] = DECAY_RATE * right_stats[slot] + (1.0 - DECAY_RATE) * gram_right
-        return carry
-
-    lax.fori_loop(0, CAP // 2, statistics, 0)
+
+    send_answers(GROUPS - 1, 0)
+    for group in range(GROUPS):
+        send_answers(group, 1)
 
     wait_bytes(sums.at[pl.ds(0, N - 1)], sum_sems.at[0])
     totals[LAYERS - 1] = jnp.sum(sums[...], axis=0)
@@ -284,7 +267,35 @@
             device_id={"layer": (layer + offset) % LAYERS},
             device_id_type=MESH,
         ).start()
-    lax.fori_loop(CAP // 2, CAP, statistics, 0)
+
+    wait_bytes(arrived.at[pl.ds(0, CAP * (N - 1))], recv_sems.at[1])
+
+    def give(ref, target):
+        for block in range(BLOCKS):
+            ref[target, block] = arrived[back_table[0, target * BLOCKS + block]]
+
+    for target in targets:
+        give(homing, target)
+        remote(homing.at[target], home_ref.at[me], send_sems.at[3], recv_sems.at[2], target)
+    give(home_ref, me)
+
+    loads[5].wait()
+    loads[6].wait()
+
+    def statistics(slot, carry):
+        block = owned[slot]
+        gram_left = lax.dot_general(
+            block, block, (((1,), (1,)), ((), ())), preferred_element_type=jnp.float32
+        )
+        gram_right = lax.dot_general(
+            block, block, (((0,), (0,)), ((), ())), preferred_element_type=jnp.float32
+        )
+        new_left_ref[slot] = DECAY_RATE * left_stats[slot] + (1.0 - DECAY_RATE) * gram_left
+        new_right_ref[slot] = DECAY_RATE * right_stats[slot] + (1.0 - DECAY_RATE) * gram_right
+        return carry
+
+    lax.fori_loop(0, CAP, statistics, 0)
+
 
     wait_bytes(totals.at[pl.ds(0, LAYERS - 1)], sum_sems.at[1])
     norms_ref[BLOCKS] = jnp.sum(totals[...], axis=0)
@@ -313,7 +324,7 @@
             pltpu.VMEM((CAP, BS, BS), f32),
             pltpu.VMEM((CAP, BS, BS), f32),
             pltpu.VMEM((N, BLOCKS, ROWS, LANES), bf16),
-            pltpu.VMEM((BLOCKS + 1, 8, LANES), f32),
+            pltpu.VMEM((BLOCKS + 1, 1, LANES), f32),
         ),
         in_specs=[hbm] * len(operands),
         out_specs=(vmem,) * 4,
@@ -333,8 +344,8 @@
             pltpu.VMEM((GROUPS, N, PER, ROWS, LANES), bf16),
             pltpu.VMEM((N * CAP, ROWS, LANES), bf16),
             pltpu.VMEM((N, BLOCKS, ROWS, LANES), bf16),
-            pltpu.VMEM((N, 8, LANES), f32),
-            pltpu.VMEM((LAYERS, 8, LANES), f32),
+            pltpu.VMEM((N, 1, LANES), f32),
+            pltpu.VMEM((LAYERS, 1, LANES), f32),
             pltpu.VMEM((1, N * CAP), jnp.int32),
             pltpu.VMEM((1, NB), jnp.int32),
             pltpu.SMEM((1, N * CAP), jnp.int32),
@@ -365,11 +376,11 @@
     for out in outs:
         out.start()
     entries = float(LAYERS * NB * BS * BS)
-    clip_factor = jnp.minimum(1.0, UPDATE_RMS / jnp.sqrt(norms_ref[BLOCKS, :1, :] / entries))
+    clip_factor = jnp.minimum(1.0, UPDATE_RMS / jnp.sqrt(norms_ref[BLOCKS] / entries))
     for block in range(BLOCKS):
         pre = home_ref[:, block].astype(jnp.float32)
         pre_sq = jnp.full((1, LANES), jnp.sum(pre * pre), jnp.float32)
-        ratio = jnp.sqrt(norms_ref[block, :1, :] / float(BS * BS)) / jnp.sqrt(
+        ratio = jnp.sqrt(norms_ref[block] / float(BS * BS)) / jnp.sqrt(
             pre_sq / float(BS * BS) + NORM_FLOOR
         )
         factor = ratio * clip_factor

time: 73.9 us -> 71.3 us (0.965)
  Pallas kernels: 73.1 us -> 70.5 us
    pallas_call x1, Pallas kernels: 70.1 us -> 67.5 us  [routed(): pl.pallas_call(routed_kernel, out_shape=(pltpu.VMEM((CAP, BS, BS), f32),...]
where the time goes in v3:
time: 71.3 us; the launch traced here: 71.2 us
  Pallas kernels  70.5 us (99%)
    pallas_call x1, Pallas kernels, routed(): pl.pallas_call(routed_kernel, out_shape=(pltpu.VMEM((CAP, BS, BS), f32),...  67.5 us
    pallas_call x1, Pallas kernels, finish(): pl.pallas_call(finish_kernel, out_shape=(jax.ShapeDtypeStruct((1, BLOCKS,...  3.07 us

profile of v3, /device:TPU:1, one launch (start us, length us, event | category | flops | bytes accessed | tf_op | source)
XLA Modules:
  0.0 71.2 jit_solution(14404443281635393984)
XLA Ops:
  0.6 67.5 %route_blocks.1 = (f32[12,256,256]{2,1,0:T(8,128)S(1)}, f32[12,256,256]{2,1,0:T(8,128)S(1)}, bf16[32,8,16,128]{3,2,1,0:T(8,128)(2,1)S(1)}, f32[9,1,128]{2,1,0:T(1,128)S(1)}) custom-call(s32[1,256]{1,0:T(1,128)} %bitcast.1, bf16[1,8,256,256]{3,2,1,0:T(8,128)(2,1)} %grad_ref.1, f32[1,8,256,256]{3,2,1,0:T(8,128)} %second_ref.1, ...), custom_call_target="tpu_custom_call" | custom-call | flops 1610612736 | bytes 18874368 | tf_op jit(solution)/shard_map/route_blocks/pallas_call | solution.py:321
  68.1 3.1 %write_results.1 = (bf16[1,8,256,256]{3,2,1,0:T(8,128)(2,1)}, f32[1,12,256,256]{3,2,1,0:T(8,128)}, f32[1,12,256,256]{3,2,1,0:T(8,128)}) custom-call(f32[12,256,256]{2,1,0:T(8,128)S(1)} %get-tuple-element.7.left_ref, f32[12,256,256]{2,1,0:T(8,128)S(1)} %get-tuple-element.8.right_ref, bf16[32,8,16,128]{3,2,1,0:T(8,128)(2,1)S(1)} %get-tuple-element.9.home_ref, ...), custom_call_target="tpu_custom_call" | custom-call | flops 3145728 | bytes 14680064 | tf_op jit(solution)/shard_map/write_results/pallas_call | solution.py:398

commit v4 on v3

--- a/solution.py
+++ b/solution.py
@@ -26,21 +26,16 @@
 MIB = 2**20
 
 
-def hops(step):
-    dz, dx, _ = step
-    return min(dz, RING - dz) + min(dx, RING - dx)
-
-
-STEPS = sorted(
-    (
-        (dz, dx, dc)
-        for dz in range(RING)
-        for dx in range(RING)
-        for dc in range(CORES)
-        if (dz, dx, dc) != (0, 0, 0)
-    ),
-    key=lambda step: (-hops(step), step[2], min(step[0], RING - step[0]), step),
+PLACES = (
+    ((2, 2),),
+    ((0, 2), (2, 0)),
+    ((1, 2), (2, 3), (3, 2), (2, 1)),
+    ((1, 1), (3, 3), (1, 3), (3, 1)),
+    ((0, 1), (1, 0), (0, 3), (3, 0)),
 )
+STEPS = [
+    (dz, dx, dc) for alike in PLACES for dc in range(CORES) for dz, dx in alike
+] + [(0, 0, 1)]
 
 
 def partner(me, step):
@@ -107,18 +102,6 @@
     me = lax.axis_index("fsdp")
     layer = lax.axis_index("layer")
 
-    barrier = pltpu.get_barrier_semaphore()
-    for step in STEPS:
-        pl.semaphore_signal(
-            barrier, inc=1, device_id={"fsdp": partner(me, step)}, device_id_type=MESH
-        )
-    for offset in range(1, LAYERS):
-        pl.semaphore_signal(
-            barrier,
-            inc=1,
-            device_id={"layer": (layer + offset) % LAYERS},
-            device_id_type=MESH,
-        )
     loads = [
         pltpu.make_async_copy(src, dst, load_sems.at[index])
         for index, (src, dst) in enumerate(
@@ -135,6 +118,18 @@
     ]
     loads[0].start()
     loads[1].start()
+    barrier = pltpu.get_barrier_semaphore()
+    for step in STEPS:
+        pl.semaphore_signal(
+            barrier, inc=1, device_id={"fsdp": partner(me, step)}, device_id_type=MESH
+        )
+    for offset in range(1, LAYERS):
+        pl.semaphore_signal(
+            barrier,
+            inc=1,
+            device_id={"layer": (layer + offset) % LAYERS},
+            device_id_type=MESH,
+        )
     loads[0].wait()
     pl.semaphore_wait(barrier, N - 1 + LAYERS - 1)
 

time: 71.3 us -> 70.5 us (0.989)
  Pallas kernels: 70.5 us -> 69.7 us
    pallas_call x1, Pallas kernels: 67.5 us -> 66.6 us  [routed(): pl.pallas_call(routed_kernel, out_shape=(pltpu.VMEM((CAP, BS, BS), f32),...]
where the time goes in v4:
time: 70.5 us; the launch traced here: 70.3 us
  Pallas kernels  69.7 us (99%)
    pallas_call x1, Pallas kernels, routed(): pl.pallas_call(routed_kernel, out_shape=(pltpu.VMEM((CAP, BS, BS), f32),...  66.6 us
    pallas_call x1, Pallas kernels, finish(): pl.pallas_call(finish_kernel, out_shape=(jax.ShapeDtypeStruct((1, BLOCKS,...  3.07 us

profile of v4, /device:TPU:1, one launch (start us, length us, event | category | flops | bytes accessed | tf_op | source)
XLA Modules:
  0.0 70.3 jit_solution(16359691283263159562)
XLA Ops:
  0.6 66.6 %route_blocks.1 = (f32[12,256,256]{2,1,0:T(8,128)S(1)}, f32[12,256,256]{2,1,0:T(8,128)S(1)}, bf16[32,8,16,128]{3,2,1,0:T(8,128)(2,1)S(1)}, f32[9,1,128]{2,1,0:T(1,128)S(1)}) custom-call(s32[1,256]{1,0:T(1,128)} %bitcast.1, bf16[1,8,256,256]{3,2,1,0:T(8,128)(2,1)} %grad_ref.1, f32[1,8,256,256]{3,2,1,0:T(8,128)} %second_ref.1, ...), custom_call_target="tpu_custom_call" | custom-call | flops 1610612736 | bytes 18874368 | tf_op jit(solution)/shard_map/route_blocks/pallas_call | solution.py:316
  67.3 3.1 %write_results.1 = (bf16[1,8,256,256]{3,2,1,0:T(8,128)(2,1)}, f32[1,12,256,256]{3,2,1,0:T(8,128)}, f32[1,12,256,256]{3,2,1,0:T(8,128)}) custom-call(f32[12,256,256]{2,1,0:T(8,128)S(1)} %get-tuple-element.7.left_ref, f32[12,256,256]{2,1,0:T(8,128)S(1)} %get-tuple-element.8.right_ref, bf16[32,8,16,128]{3,2,1,0:T(8,128)(2,1)S(1)} %get-tuple-element.9.home_ref, ...), custom_call_target="tpu_custom_call" | custom-call | flops 3145728 | bytes 14680064 | tf_op jit(solution)/shard_map/write_results/pallas_call | solution.py:393

commit v5 on v4

--- a/solution.py
+++ b/solution.py
@@ -29,8 +29,8 @@
 PLACES = (
     ((2, 2),),
     ((0, 2), (2, 0)),
+    ((1, 1), (3, 3), (1, 3), (3, 1)),
     ((1, 2), (2, 3), (3, 2), (2, 1)),
-    ((1, 1), (3, 3), (1, 3), (3, 1)),
     ((0, 1), (1, 0), (0, 3), (3, 0)),
 )
 STEPS = [

time: 70.5 us -> 70.1 us (level)
  no operation moved by 1% of the time
where the time goes in v5:
time: 70.1 us; the launch traced here: 69.9 us
  Pallas kernels  69.3 us (99%)
    pallas_call x1, Pallas kernels, routed(): pl.pallas_call(routed_kernel, out_shape=(pltpu.VMEM((CAP, BS, BS), f32),...  66.2 us
    pallas_call x1, Pallas kernels, finish(): pl.pallas_call(finish_kernel, out_shape=(jax.ShapeDtypeStruct((1, BLOCKS,...  3.07 us

profile of v5, /device:TPU:1, one launch (start us, length us, event | category | flops | bytes accessed | tf_op | source)
XLA Modules:
  0.0 69.9 jit_solution(10073719657292385342)
XLA Ops:
  0.6 66.2 %route_blocks.1 = (f32[12,256,256]{2,1,0:T(8,128)S(1)}, f32[12,256,256]{2,1,0:T(8,128)S(1)}, bf16[32,8,16,128]{3,2,1,0:T(8,128)(2,1)S(1)}, f32[9,1,128]{2,1,0:T(1,128)S(1)}) custom-call(s32[1,256]{1,0:T(1,128)} %bitcast.1, bf16[1,8,256,256]{3,2,1,0:T(8,128)(2,1)} %grad_ref.1, f32[1,8,256,256]{3,2,1,0:T(8,128)} %second_ref.1, ...), custom_call_target="tpu_custom_call" | custom-call | flops 1610612736 | bytes 18874368 | tf_op jit(solution)/shard_map/route_blocks/pallas_call | solution.py:316
  66.9 3.1 %write_results.1 = (bf16[1,8,256,256]{3,2,1,0:T(8,128)(2,1)}, f32[1,12,256,256]{3,2,1,0:T(8,128)}, f32[1,12,256,256]{3,2,1,0:T(8,128)}) custom-call(f32[12,256,256]{2,1,0:T(8,128)S(1)} %get-tuple-element.7.left_ref, f32[12,256,256]{2,1,0:T(8,128)S(1)} %get-tuple-element.8.right_ref, bf16[32,8,16,128]{3,2,1,0:T(8,128)(2,1)S(1)} %get-tuple-element.9.home_ref, ...), custom_call_target="tpu_custom_call" | custom-call | flops 3145728 | bytes 14680064 | tf_op jit(solution)/shard_map/write_results/pallas_call | solution.py:393

commit v6 on v5

--- a/solution.py
+++ b/solution.py
@@ -167,6 +167,26 @@
     ]
     for table in tables:
         table.start()
+    for table in tables:
+        table.wait()
+    wait_bytes(spread.at[pl.ds(0, NB - BLOCKS)], recv_sems.at[0])
+
+    def take(ref, group, target):
+        for slot in range(PER):
+            ref[group, target, slot] = spread[take_table[0, target * CAP + group * PER + slot]]
+
+    for group in range(GROUPS):
+        for target in targets:
+            take(outgo, group, target)
+            remote(
+                outgo.at[group, target],
+                landed.at[group, me],
+                send_sems.at[1],
+                route_sems.at[group],
+                target,
+            )
+        take(landed, group, me)
+
     loads[2].wait()
 
     def adam_block(b, total):
@@ -184,26 +204,6 @@
         return total + block_sum
 
     sums[N - 1] = lax.fori_loop(0, BLOCKS, adam_block, jnp.zeros((1, LANES), jnp.float32))
-
-    for table in tables:
-        table.wait()
-    wait_bytes(spread.at[pl.ds(0, NB - BLOCKS)], recv_sems.at[0])
-
-    def take(ref, group, target):
-        for slot in range(PER):
-            ref[group, target, slot] = spread[take_table[0, target * CAP + group * PER + slot]]
-
-    for group in range(GROUPS):
-        for target in targets:
-            take(outgo, group, target)
-            remote(
-                outgo.at[group, target],
-                landed.at[group, me],
-                send_sems.at[1],
-                route_sems.at[group],
-                target,
-            )
-        take(landed, group, me)
 
     for index, target in enumerate(targets):
         remote(sums.at[N - 1], sums.at[index], send_sems.at[4], sum_sems.at[0], target)

time: 70.1 us -> 70.1 us (level)
  no operation moved by 1% of the time
where the time goes in v6:
time: 70.1 us; the launch traced here: 69.9 us
  Pallas kernels  69.3 us (99%)
    pallas_call x1, Pallas kernels, routed(): pl.pallas_call(routed_kernel, out_shape=(pltpu.VMEM((CAP, BS, BS), f32),...  66.2 us
    pallas_call x1, Pallas kernels, finish(): pl.pallas_call(finish_kernel, out_shape=(jax.ShapeDtypeStruct((1, BLOCKS,...  3.07 us

profile of v6, /device:TPU:1, one launch (start us, length us, event | category | flops | bytes accessed | tf_op | source)
XLA Modules:
  0.0 69.9 jit_solution(5057394695975291370)
XLA Ops:
  0.6 66.2 %route_blocks.1 = (f32[12,256,256]{2,1,0:T(8,128)S(1)}, f32[12,256,256]{2,1,0:T(8,128)S(1)}, bf16[32,8,16,128]{3,2,1,0:T(8,128)(2,1)S(1)}, f32[9,1,128]{2,1,0:T(1,128)S(1)}) custom-call(s32[1,256]{1,0:T(1,128)} %bitcast.1, bf16[1,8,256,256]{3,2,1,0:T(8,128)(2,1)} %grad_ref.1, f32[1,8,256,256]{3,2,1,0:T(8,128)} %second_ref.1, ...), custom_call_target="tpu_custom_call" | custom-call | flops 1610612736 | bytes 18874368 | tf_op jit(solution)/shard_map/route_blocks/pallas_call | solution.py:316
  66.9 3.1 %write_results.1 = (bf16[1,8,256,256]{3,2,1,0:T(8,128)(2,1)}, f32[1,12,256,256]{3,2,1,0:T(8,128)}, f32[1,12,256,256]{3,2,1,0:T(8,128)}) custom-call(f32[12,256,256]{2,1,0:T(8,128)S(1)} %get-tuple-element.7.left_ref, f32[12,256,256]{2,1,0:T(8,128)S(1)} %get-tuple-element.8.right_ref, bf16[32,8,16,128]{3,2,1,0:T(8,128)(2,1)S(1)} %get-tuple-element.9.home_ref, ...), custom_call_target="tpu_custom_call" | custom-call | flops 3145728 | bytes 14680064 | tf_op jit(solution)/shard_map/write_results/pallas_call | solution.py:393
